TPU v7x, 1024 devices: a whole 4x8x16 slice. The times are simulated.
1024 devices in a mesh: dp: 16 (over y, core), expert: 64 (over x, z).
Axes of the slice: x: 4, y: 8, z: 16, core: 2. Of those that a mesh axis runs over, the one named last changes fastest.
Arguments:
- tokens: bfloat16 [131072, 512], P(('dp', 'expert')), may hold values from -40 to 40
- norm_gain: float32 [512], replicated, may hold values from 0.5 to 1.5
- routes: int32 [131072, 2], P(('dp', 'expert')), may hold values from 0 to 63, all different within a row; in each aligned block of 128 rows (0 to 127, 128 to 255, ...) at most 5 rows name the same one
- gate_weights: float32 [131072, 2], P(('dp', 'expert')), may hold values from 0.05 to 1
- weight_in: bfloat16 [64, 2048, 512], P('expert'), may hold values from -0.25 to 0.25
- weight_out: bfloat16 [64, 2048, 512], P('expert'), may hold values from -0.125 to 0.125
- out_grad: bfloat16 [131072, 512], P(('dp', 'expert')), may hold values from -1.5 to 1.5
Outputs:
- mixed: bfloat16 [131072, 512], P(('dp', 'expert'))
- gate_grad: float32 [131072, 2], P(('dp', 'expert'))
- token_grad: bfloat16 [131072, 512], P(('dp', 'expert'))
- w_in_grad: float32 [64, 2048, 512], P('expert', 'dp')
- w_out_grad: float32 [64, 2048, 512], P('expert', 'dp')
Inputs may be any that keep to these rules, and one draw needn't show every extreme that they name: `routes`: each frame names 2 different experts; among the frames of one device no expert is named more than 5 times.
All inputs are finite; a program needn't handle non-finite values.
Results may differ from a plain program's by a relative error of at most 0.022.
Values may be sent and summed in bfloat16 or wider, within the bound.
A program may use at most 64 MiB of HBM per device.

v0:
```python
from functools import partial
import math

import jax
import jax.numpy as jnp
from jax import lax
from jax.sharding import PartitionSpec as P

epsilon = 1e-05


def swish_parts(hidden_v):
    sigmoid_v = jax.nn.sigmoid(hidden_v)
    return (hidden_v * sigmoid_v, sigmoid_v * (1.0 + hidden_v * (1.0 - sigmoid_v)))


def row_slots(flat_exp, n_experts):
    onehot = (flat_exp[:, None] == jnp.arange(n_experts, dtype=jnp.int32)[None, :]).astype(
        jnp.int32
    )
    before = jnp.cumsum(onehot, axis=0) - onehot
    return (jnp.sum(before * onehot, axis=1), jnp.sum(onehot, axis=0))


def expert_blocks(rows_in, rows_cot, weight_in, weight_out, n_blocks, block_rows):
    slot_total, model_dim = rows_in.shape
    hidden_dim = weight_in.shape[0]
    contract_dims = (((1,), (1,)), ((), ()))

    def expert_step(block_idx, carry):
        activ, hid_grads, expert_out, expert_ingrad = carry
        first_row = block_idx * block_rows
        in_blk = lax.dynamic_slice_in_dim(rows_in, first_row, block_rows, 0)
        cot_blk = lax.dynamic_slice_in_dim(rows_cot, first_row, block_rows, 0)
        pre_act = lax.dot_general(
            in_blk, weight_in, contract_dims, preferred_element_type=jnp.float32
        )
        act_full, derivative = swish_parts(pre_act)
        act_half = act_full.astype(jnp.bfloat16)
        out_blk = jnp.dot(act_half, weight_out, preferred_element_type=jnp.float32).astype(
            jnp.bfloat16
        )
        back_prod = lax.dot_general(
            cot_blk, weight_out, contract_dims, preferred_element_type=jnp.float32
        )
        hid_grad = (back_prod * derivative).astype(jnp.bfloat16)
        in_grad = jnp.dot(hid_grad, weight_in, preferred_element_type=jnp.float32).astype(
            jnp.bfloat16
        )
        return (
            lax.dynamic_update_slice_in_dim(activ, act_half, first_row, 0),
            lax.dynamic_update_slice_in_dim(hid_grads, hid_grad, first_row, 0),
            lax.dynamic_update_slice_in_dim(expert_out, out_blk, first_row, 0),
            lax.dynamic_update_slice_in_dim(expert_ingrad, in_grad, first_row, 0),
        )

    start_state = (
        jnp.zeros((slot_total, hidden_dim), jnp.bfloat16),
        jnp.zeros((slot_total, hidden_dim), jnp.bfloat16),
        jnp.zeros((slot_total, model_dim), jnp.bfloat16),
        jnp.zeros((slot_total, model_dim), jnp.bfloat16),
    )
    return lax.fori_loop(0, n_blocks, expert_step, start_state)


def weight_terms(activ, hid_grads, rows_in, rows_cot, n_blocks, block_rows, start, count):
    contract_dims = (((0,), (0,)), ((), ()))
    model_dim = rows_in.shape[1]
    first_col = jnp.asarray(start)

    def weight_step(block_idx, sums):
        first_row = (block_idx * block_rows).astype(jnp.int32)
        grad_part = lax.dynamic_slice(hid_grads, (first_row, first_col), (block_rows, count))
        act_part = lax.dynamic_slice(activ, (first_row, first_col), (block_rows, count))
        in_blk = lax.dynamic_slice_in_dim(rows_in, first_row, block_rows, 0)
        cot_blk = lax.dynamic_slice_in_dim(rows_cot, first_row, block_rows, 0)
        grad_in = lax.dot_general(
            grad_part, in_blk, contract_dims, preferred_element_type=jnp.float32
        )
        grad_out = lax.dot_general(
            act_part, cot_blk, contract_dims, preferred_element_type=jnp.float32
        )
        return (sums[0] + grad_in, sums[1] + grad_out)

    zeros_start = (
        jnp.zeros((count, model_dim), jnp.float32),
        jnp.zeros((count, model_dim), jnp.float32),
    )
    sum_in, sum_out = lax.fori_loop(0, n_blocks, weight_step, zeros_start)
    return jnp.concatenate([sum_in, sum_out], axis=1)


def local(tokens, norm_gain, routes, gate_weights, weight_in, weight_out, out_grad):
    n_experts = lax.axis_size("expert")
    frame_count, model_dim = tokens.shape
    n_routes = routes.shape[1]
    capacity = max(2, 5 * frame_count // (2 * n_experts))
    slot_total = n_experts * capacity
    block_rows = math.gcd(32, slot_total)
    values = tokens.astype(jnp.float32)
    centered = values - jnp.mean(values, axis=1, keepdims=True)
    inv_std = lax.rsqrt(jnp.mean(centered * centered, axis=1, keepdims=True) + epsilon)
    standard = centered * inv_std
    normed = (standard * norm_gain).astype(jnp.bfloat16)
    flat_exp = routes.reshape(-1)
    slot_of, per_expert = row_slots(flat_exp, n_experts)
    dest_row = flat_exp * capacity + slot_of
    route_in = jnp.repeat(normed, n_routes, axis=0)
    route_cot = (
        (gate_weights[:, :, None] * out_grad.astype(jnp.float32)[:, None, :])
        .astype(jnp.bfloat16)
        .reshape(frame_count * n_routes, model_dim)
    )
    send_in = (
        jnp.zeros((slot_total, model_dim), jnp.bfloat16)
        .at[dest_row]
        .set(route_in)
        .reshape(n_experts, capacity, model_dim)
    )
    send_cot = (
        jnp.zeros((slot_total, model_dim), jnp.bfloat16)
        .at[dest_row]
        .set(route_cot)
        .reshape(n_experts, capacity, model_dim)
    )
    expert_win = weight_in[0]
    expert_wout = weight_out[0]
    got_in, got_cot, got_counts = (
        lax.all_to_all(send_in, "expert", split_axis=0, concat_axis=0, tiled=True),
        lax.all_to_all(send_cot, "expert", split_axis=0, concat_axis=0, tiled=True),
        lax.all_to_all(
            per_expert.reshape(n_experts, 1), "expert", split_axis=0, concat_axis=0, tiled=True
        ),
    )
    live_counts = got_counts[:, 0]
    offsets = jnp.cumsum(live_counts) - live_counts
    in_slot = jnp.arange(capacity, dtype=jnp.int32)
    is_live = (in_slot[None, :] < live_counts[:, None]).reshape(-1)
    place_at = (offsets[:, None] + in_slot[None, :]).reshape(-1)
    drop_at = jnp.where(is_live, place_at, slot_total)
    rows_in = (
        jnp.zeros((slot_total, model_dim), jnp.bfloat16)
        .at[drop_at]
        .set(got_in.reshape(slot_total, model_dim), mode="drop")
    )
    rows_cot = (
        jnp.zeros((slot_total, model_dim), jnp.bfloat16)
        .at[drop_at]
        .set(got_cot.reshape(slot_total, model_dim), mode="drop")
    )
    n_blocks = (jnp.sum(live_counts) + block_rows - 1) // block_rows
    activ, hid_grads, expert_out, expert_ingrad = expert_blocks(
        rows_in, rows_cot, expert_win, expert_wout, n_blocks, block_rows
    )
    pick_row = jnp.minimum(place_at, slot_total - 1)
    nothing = jnp.zeros((), jnp.bfloat16)
    back_y = jnp.where(is_live[:, None], expert_out[pick_row], nothing).reshape(
        n_experts, capacity, model_dim
    )
    back_du = jnp.where(is_live[:, None], expert_ingrad[pick_row], nothing).reshape(
        n_experts, capacity, model_dim
    )
    hid_share = expert_win.shape[0] // lax.axis_size("dp")
    term_maker = partial(weight_terms, activ, hid_grads, rows_in, rows_cot, n_blocks, block_rows)
    ret_y, ret_du = (
        lax.all_to_all(back_y, "expert", split_axis=0, concat_axis=0, tiled=True),
        lax.all_to_all(back_du, "expert", split_axis=0, concat_axis=0, tiled=True),
    )
    summed = lax.psum_scatter(
        term_maker(jnp.int32(0), lax.axis_size("dp") * hid_share).astype(jnp.bfloat16),
        "dp",
        scatter_dimension=0,
        tiled=True,
    ).astype(jnp.float32)
    y_rows = ret_y.reshape(slot_total, model_dim)[dest_row].reshape(
        frame_count, n_routes, model_dim
    )
    du_rows = ret_du.reshape(slot_total, model_dim)[dest_row].reshape(
        frame_count, n_routes, model_dim
    )
    mixed = jnp.sum(gate_weights[:, :, None] * y_rows.astype(jnp.float32), axis=1).astype(
        jnp.bfloat16
    )
    gate_grad = jnp.einsum("td,tkd->tk", out_grad.astype(jnp.float32), y_rows.astype(jnp.float32))
    norm_grad = jnp.sum(du_rows.astype(jnp.float32), axis=1) * norm_gain
    token_grad = inv_std * (
        norm_grad
        - jnp.mean(norm_grad, axis=1, keepdims=True)
        - standard * jnp.mean(norm_grad * standard, axis=1, keepdims=True)
    )
    w_in_grad = summed[:, :model_dim][None]
    w_out_grad = summed[:, model_dim:][None]
    return (mixed, gate_grad, token_grad.astype(jnp.bfloat16), w_in_grad, w_out_grad)


def solution(mesh):
    placed = (
        P(("dp", "expert"), None),
        P(),
        P(("dp", "expert"), None),
        P(("dp", "expert"), None),
        P("expert", None, None),
        P("expert", None, None),
        P(("dp", "expert"), None),
    )
    return jax.shard_map(
        local,
        mesh=mesh,
        in_specs=placed,
        out_specs=(
            P(("dp", "expert"), None),
            P(("dp", "expert"), None),
            P(("dp", "expert"), None),
            P("expert", "dp", None),
            P("expert", "dp", None),
        ),
        check_vma=False,
    )
```

profile of v0, /device:TPU:1, one launch (start us, length us, event | category | flops | bytes accessed | tf_op | source)
XLA Modules:
  0.0 358.7 jit_solution(16212597269415256353)
XLA Ops:
  10.0 22.8 %all-to-all-start = ((s32[64,1,1]{2,1,0:T(1,128)}), s32[64,1,1]{2,1,0:T(1,128)S(1)}, u32[]{:S(2)}, u32[]{:S(2)}) async-start(s32[64,1,1]{2,1,0:T(1,128)} %copy.31), calls=%async_computation | async-start | bytes 65536 | tf_op jit(solution)/shard_map/all_to_all | solution.py:131
  37.1 1.6 scatter_custom_fusion
  39.6 6.3 %all-to-all-done = s32[64,1,1]{2,1,0:T(1,128)S(1)} async-done(((s32[64,1,1]{2,1,0:T(1,128)}), s32[64,1,1]{2,1,0:T(1,128)S(1)}, u32[]{:S(2)}, u32[]{:S(2)}) %all-to-all-start) | async-done | bytes 288 | tf_op jit(solution)/shard_map/all_to_all | solution.py:131
  46.0 8.2 %all-to-all-start.1 = ((bf16[64,5,512]{2,1,0:T(8,128)(2,1)}), bf16[64,5,512]{2,1,0:T(8,128)(2,1)S(1)}, u32[]{:S(2)}, u32[]{:S(2)}) async-start(bf16[64,5,512]{2,1,0:T(8,128)(2,1)} %reshape.246), calls=%async_computation.1 | async-start | bytes 1048576 | tf_op jit(solution)/shard_map/all_to_all | solution.py:129
  55.0 1.7 scatter_custom_fusion.2
  57.6 25.5 %all-to-all-done.1 = bf16[64,5,512]{2,1,0:T(8,128)(2,1)S(1)} async-done(((bf16[64,5,512]{2,1,0:T(8,128)(2,1)}), bf16[64,5,512]{2,1,0:T(8,128)(2,1)S(1)}, u32[]{:S(2)}, u32[]{:S(2)}) %all-to-all-start.1) | async-done | bytes 327712 | tf_op jit(solution)/shard_map/all_to_all | solution.py:129
  83.1 9.1 %all-to-all-start.2 = ((bf16[64,5,512]{2,1,0:T(8,128)(2,1)}), bf16[64,5,512]{2,1,0:T(8,128)(2,1)S(1)}, u32[]{:S(2)}, u32[]{:S(2)}) async-start(bf16[64,5,512]{2,1,0:T(8,128)(2,1)} %reshape.248), calls=%async_computation.2 | async-start | bytes 1048576 | tf_op jit(solution)/shard_map/all_to_all | solution.py:130
  92.2 1.8 fusion.43
  95.3 1.8 scatter_custom_fusion.1
  97.1 24.1 %all-to-all-done.2 = bf16[64,5,512]{2,1,0:T(8,128)(2,1)S(1)} async-done(((bf16[64,5,512]{2,1,0:T(8,128)(2,1)}), bf16[64,5,512]{2,1,0:T(8,128)(2,1)S(1)}, u32[]{:S(2)}, u32[]{:S(2)}) %all-to-all-start.2) | async-done | bytes 327712 | tf_op jit(solution)/shard_map/all_to_all | solution.py:130
  122.1 2.2 scatter_custom_fusion.3
  127.0 26.8 %while.28 = (s32[]{:T(128)}, bf16[320,2048]{1,0:T(8,128)(2,1)}, bf16[320,2048]{1,0:T(8,128)(2,1)}, bf16[320,512]{1,0:T(8,128)(2,1)S(1)}, bf16[320,512]{1,0:T(8,1...) while((s32[]{:T(128)}, bf16[320,2048]{1,0:T(8,128)(2,1)}, ...), condition=%wide.region_13.14_spmd, body=%wide.region_12.13_spmd.sunk | while | flops 269713408 | bytes 18221272 | solution.py:63
  134.6 1.4 constant_dynamic-update-slice_fusion.4
  142.3 1.4 constant_dynamic-update-slice_fusion.4
  146.1 1.4 constant_dynamic-update-slice_fusion.4
  150.0 1.4 constant_dynamic-update-slice_fusion.4
  153.8 2.5 broadcast.168.clone
  156.3 2.5 broadcast.168
  158.8 60.7 %while.29 = (s32[]{:T(128)}, f32[2048,512]{1,0:T(8,128)}, f32[2048,512]{1,0:T(8,128)}, s32[]{:T(128)}, bf16[320,2048]{1,0:T(8,128)(2,1)}, /*index=5*/bf16[320,51...) while((s32[]{:T(128)}, f32[2048,512]{1,0:T(8,128)}, ...), condition=%wide.region_19.20_spmd, body=%wide.region_18.19_spmd.sunk | while | flops 136314880 | bytes 50661592 | solution.py:89
  158.8 5.1 %convolution_add_fusion.5 = f32[2048,512]{1,0:T(8,128)} fusion(f32[2048,512]{1,0:T(8,128)} %get-tuple-element.341, bf16[320,2048]{1,0:T(8,128)(2,1)} %get-tuple-element.357, s32[]{:T(128)S(6)} %select_n.98, bf16[320,512]{1,0:T(8,128)(2,1)S(1)} %get-tuple-element.358), kind=kOutput, calls=%fused_computation.23.clone.1 | convolution fusion | flops 68157440 | bytes 8553472 | tf_op jit(solution)/shard_map/while/body/dot_general | solution.py:80
  163.9 1.6 convolution_add_fusion.4
  165.6 1.9 copy-done.2
  167.5 5.1 %convolution_add_fusion.5 = f32[2048,512]{1,0:T(8,128)} fusion(f32[2048,512]{1,0:T(8,128)} %get-tuple-element.341, bf16[320,2048]{1,0:T(8,128)(2,1)} %get-tuple-element.357, s32[]{:T(128)S(6)} %select_n.98, bf16[320,512]{1,0:T(8,128)(2,1)S(1)} %get-tuple-element.358), kind=kOutput, calls=%fused_computation.23.clone.1 | convolution fusion | flops 68157440 | bytes 8553472 | tf_op jit(solution)/shard_map/while/body/dot_general | solution.py:80
  172.6 1.6 convolution_add_fusion.4
  174.2 1.9 copy-done.2
  176.1 5.1 %convolution_add_fusion.5 = f32[2048,512]{1,0:T(8,128)} fusion(f32[2048,512]{1,0:T(8,128)} %get-tuple-element.341, bf16[320,2048]{1,0:T(8,128)(2,1)} %get-tuple-element.357, s32[]{:T(128)S(6)} %select_n.98, bf16[320,512]{1,0:T(8,128)(2,1)S(1)} %get-tuple-element.358), kind=kOutput, calls=%fused_computation.23.clone.1 | convolution fusion | flops 68157440 | bytes 8553472 | tf_op jit(solution)/shard_map/while/body/dot_general | solution.py:80
  181.3 1.6 convolution_add_fusion.4
  182.9 1.9 copy-done.2
  184.8 5.1 %convolution_add_fusion.5 = f32[2048,512]{1,0:T(8,128)} fusion(f32[2048,512]{1,0:T(8,128)} %get-tuple-element.341, bf16[320,2048]{1,0:T(8,128)(2,1)} %get-tuple-element.357, s32[]{:T(128)S(6)} %select_n.98, bf16[320,512]{1,0:T(8,128)(2,1)S(1)} %get-tuple-element.358), kind=kOutput, calls=%fused_computation.23.clone.1 | convolution fusion | flops 68157440 | bytes 8553472 | tf_op jit(solution)/shard_map/while/body/dot_general | solution.py:80
  189.9 1.6 convolution_add_fusion.4
  191.6 1.9 copy-done.2
  193.5 5.1 %convolution_add_fusion.5 = f32[2048,512]{1,0:T(8,128)} fusion(f32[2048,512]{1,0:T(8,128)} %get-tuple-element.341, bf16[320,2048]{1,0:T(8,128)(2,1)} %get-tuple-element.357, s32[]{:T(128)S(6)} %select_n.98, bf16[320,512]{1,0:T(8,128)(2,1)S(1)} %get-tuple-element.358), kind=kOutput, calls=%fused_computation.23.clone.1 | convolution fusion | flops 68157440 | bytes 8553472 | tf_op jit(solution)/shard_map/while/body/dot_general | solution.py:80
  198.6 1.6 convolution_add_fusion.4
  200.2 1.9 copy-done.2
  202.2 5.1 %convolution_add_fusion.5 = f32[2048,512]{1,0:T(8,128)} fusion(f32[2048,512]{1,0:T(8,128)} %get-tuple-element.341, bf16[320,2048]{1,0:T(8,128)(2,1)} %get-tuple-element.357, s32[]{:T(128)S(6)} %select_n.98, bf16[320,512]{1,0:T(8,128)(2,1)S(1)} %get-tuple-element.358), kind=kOutput, calls=%fused_computation.23.clone.1 | convolution fusion | flops 68157440 | bytes 8553472 | tf_op jit(solution)/shard_map/while/body/dot_general | solution.py:80
  207.3 1.6 convolution_add_fusion.4
  208.9 1.9 copy-done.2
  210.8 5.1 %convolution_add_fusion.5 = f32[2048,512]{1,0:T(8,128)} fusion(f32[2048,512]{1,0:T(8,128)} %get-tuple-element.341, bf16[320,2048]{1,0:T(8,128)(2,1)} %get-tuple-element.357, s32[]{:T(128)S(6)} %select_n.98, bf16[320,512]{1,0:T(8,128)(2,1)S(1)} %get-tuple-element.358), kind=kOutput, calls=%fused_computation.23.clone.1 | convolution fusion | flops 68157440 | bytes 8553472 | tf_op jit(solution)/shard_map/while/body/dot_general | solution.py:80
  215.9 1.6 convolution_add_fusion.4
  217.6 1.9 copy-done.2
  219.5 2.6 convert.8
  223.2 2.6 pad_maximum_fusion
  226.1 2.0 gather_fusion.2
  228.1 2.0 gather_fusion
  231.4 75.2 %all_to_all.29 = bf16[64,5,512]{2,1,0:T(8,128)(2,1)S(1)} all-to-all(bf16[64,5,512]{2,1,0:T(8,128)(2,1)S(1)} %get-tuple-element.159), channel_id=1, replica_groups=mesh['dp'=16,'expert'=64] {'expert'}, dimensions={0} | all-to-all | bytes 655360 | tf_op jit(solution)/shard_map/all_to_all | solution.py:167
  306.6 9.2 %all-to-all-start.3 = ((bf16[64,5,512]{2,1,0:T(8,128)(2,1)}), bf16[64,5,512]{2,1,0:T(8,128)(2,1)S(1)}, u32[]{:S(2)}, u32[]{:S(2)}) async-start(bf16[64,5,512]{2,1,0:T(8,128)(2,1)} %get-tuple-element.160), calls=%async_computation.3 | async-start | bytes 1048576 | tf_op jit(solution)/shard_map/all_to_all | solution.py:166
  317.2 26.8 %all-to-all-done.3 = bf16[64,5,512]{2,1,0:T(8,128)(2,1)S(1)} async-done(((bf16[64,5,512]{2,1,0:T(8,128)(2,1)}), bf16[64,5,512]{2,1,0:T(8,128)(2,1)S(1)}, u32[]{:S(2)}, u32[]{:S(2)}) %all-to-all-start.3) | async-done | bytes 327712 | tf_op jit(solution)/shard_map/all_to_all | solution.py:166
  347.8 1.4 multiply_reduce_fusion
  (138 shorter events, 45.2 us)
Async XLA Ops:
  8.3 46.0 %copy-start.8 = (f32[128,2]{0,1:T(2,128)S(1)}, f32[128,2]{0,1:T(2,128)}, u32[]{:S(2)}) copy-start(f32[128,2]{0,1:T(2,128)} %param.14) | copy-start | bytes 3076
  8.9 45.6 %copy-start.5 = (bf16[128,512]{1,0:T(8,128)(2,1)S(1)}, bf16[128,512]{1,0:T(8,128)(2,1)}, u32[]{:S(2)}) copy-start(bf16[128,512]{1,0:T(8,128)(2,1)} %param.17) | copy-start | bytes 393220
  10.0 36.0 %all-to-all-start = ((s32[64,1,1]{2,1,0:T(1,128)}), s32[64,1,1]{2,1,0:T(1,128)S(1)}, u32[]{:S(2)}, u32[]{:S(2)}) async-start(s32[64,1,1]{2,1,0:T(1,128)} %copy.31), calls=%async_computation | async-start | bytes 65536 | tf_op jit(solution)/shard_map/all_to_all | solution.py:131
  46.0 37.1 %all-to-all-start.1 = ((bf16[64,5,512]{2,1,0:T(8,128)(2,1)}), bf16[64,5,512]{2,1,0:T(8,128)(2,1)S(1)}, u32[]{:S(2)}, u32[]{:S(2)}) async-start(bf16[64,5,512]{2,1,0:T(8,128)(2,1)} %reshape.246), calls=%async_computation.1 | async-start | bytes 1048576 | tf_op jit(solution)/shard_map/all_to_all | solution.py:129
  83.1 38.2 %all-to-all-start.2 = ((bf16[64,5,512]{2,1,0:T(8,128)(2,1)}), bf16[64,5,512]{2,1,0:T(8,128)(2,1)S(1)}, u32[]{:S(2)}, u32[]{:S(2)}) async-start(bf16[64,5,512]{2,1,0:T(8,128)(2,1)} %reshape.248), calls=%async_computation.2 | async-start | bytes 1048576 | tf_op jit(solution)/shard_map/all_to_all | solution.py:130
  92.2 257.8 %reduce-scatter.2.cloned.1.call-start = ((), (), s32[]{:S(2)}) async-start(), calls=%async_computation.6 | async-start | bytes 4456448 | tf_op jit(solution)/shard_map/reduce_scatter | solution.py:169
  97.1 29.8 %copy-start = (bf16[1,2048,512]{2,1,0:T(8,128)(2,1)S(1)}, bf16[1,2048,512]{2,1,0:T(8,128)(2,1)}, u32[]{:S(2)}) copy-start(bf16[1,2048,512]{2,1,0:T(8,128)(2,1)} %param.15) | copy-start | bytes 6291460
  127.0 1.6 copy-start.9
  130.8 1.6 copy-start.9
  134.6 1.6 copy-start.9
  138.5 1.6 copy-start.9
  142.3 1.6 copy-start.9
  146.1 1.6 copy-start.9
  150.0 1.6 copy-start.9
  158.8 5.1 %copy-start.1 = (f32[2048,512]{1,0:T(8,128)S(1)}, f32[2048,512]{1,0:T(8,128)}, u32[]{:S(2)}) copy-start(f32[2048,512]{1,0:T(8,128)} %get-tuple-element.340) | copy-start | bytes 12582916 | tf_op jit(solution)/shard_map/while
  165.5 1.9 copy-start.2
  167.5 5.1 %copy-start.1 = (f32[2048,512]{1,0:T(8,128)S(1)}, f32[2048,512]{1,0:T(8,128)}, u32[]{:S(2)}) copy-start(f32[2048,512]{1,0:T(8,128)} %get-tuple-element.340) | copy-start | bytes 12582916 | tf_op jit(solution)/shard_map/while
  174.2 1.9 copy-start.2
  176.1 5.1 %copy-start.1 = (f32[2048,512]{1,0:T(8,128)S(1)}, f32[2048,512]{1,0:T(8,128)}, u32[]{:S(2)}) copy-start(f32[2048,512]{1,0:T(8,128)} %get-tuple-element.340) | copy-start | bytes 12582916 | tf_op jit(solution)/shard_map/while
  182.9 1.9 copy-start.2
  184.8 5.1 %copy-start.1 = (f32[2048,512]{1,0:T(8,128)S(1)}, f32[2048,512]{1,0:T(8,128)}, u32[]{:S(2)}) copy-start(f32[2048,512]{1,0:T(8,128)} %get-tuple-element.340) | copy-start | bytes 12582916 | tf_op jit(solution)/shard_map/while
  191.6 1.9 copy-start.2
  193.5 5.1 %copy-start.1 = (f32[2048,512]{1,0:T(8,128)S(1)}, f32[2048,512]{1,0:T(8,128)}, u32[]{:S(2)}) copy-start(f32[2048,512]{1,0:T(8,128)} %get-tuple-element.340) | copy-start | bytes 12582916 | tf_op jit(solution)/shard_map/while
  200.2 1.9 copy-start.2
  202.2 5.1 %copy-start.1 = (f32[2048,512]{1,0:T(8,128)S(1)}, f32[2048,512]{1,0:T(8,128)}, u32[]{:S(2)}) copy-start(f32[2048,512]{1,0:T(8,128)} %get-tuple-element.340) | copy-start | bytes 12582916 | tf_op jit(solution)/shard_map/while
  208.9 1.9 copy-start.2
  210.8 5.1 %copy-start.1 = (f32[2048,512]{1,0:T(8,128)S(1)}, f32[2048,512]{1,0:T(8,128)}, u32[]{:S(2)}) copy-start(f32[2048,512]{1,0:T(8,128)} %get-tuple-element.340) | copy-start | bytes 12582916 | tf_op jit(solution)/shard_map/while
  217.6 1.9 copy-start.2
  219.5 3.4 copy-start.3
  306.6 37.4 %all-to-all-start.3 = ((bf16[64,5,512]{2,1,0:T(8,128)(2,1)}), bf16[64,5,512]{2,1,0:T(8,128)(2,1)S(1)}, u32[]{:S(2)}, u32[]{:S(2)}) async-start(bf16[64,5,512]{2,1,0:T(8,128)(2,1)} %get-tuple-element.160), calls=%async_computation.3 | async-start | bytes 1048576 | tf_op jit(solution)/shard_map/all_to_all | solution.py:166
  317.2 28.3 %copy-start.6 = (bf16[128,512]{1,0:T(8,128)(2,1)S(1)}, bf16[128,512]{1,0:T(8,128)(2,1)}, u32[]{:S(2)}) copy-start(bf16[128,512]{1,0:T(8,128)(2,1)} %param.17) | copy-start | bytes 393220
  345.4 2.2 copy-start.4
  345.4 2.2 copy-start.7
Sparse Core Ops, SparseCore 0:
  226.0 103.3 reduce-scatter.1
where the time goes:
time: 362 us; the launch traced here: 359 us
  waiting for transfers between devices  82.8 us (23%)
  blocking collectives  75.2 us (21%)
  matrix products  73.1 us (20%)
  starting transfers between devices  49.4 us (14%)
  local copies, waits for them, and re-layouts  44.1 us (12%)
  other arithmetic  18.9 us (5%)
  between operations  15.1 us (4%)
    all_to_all x1, blocking collectives, local(): lax.all_to_all(back_du, 'expert', split_axis=0, concat_axis=0, tiled=True)  75.2 us
    dot_general x7, matrix products, weight_step(): lax.dot_general(act_part, cot_blk, contract_dims, preferred_element_type=...  35.7 us
    all_to_all x1, waiting for transfers between devices, local(): lax.all_to_all(back_y, 'expert', split_axis=0, concat_axis=0, tiled=True)  26.8 us
    all_to_all x1, waiting for transfers between devices, local(): lax.all_to_all(send_in, 'expert', split_axis=0, concat_axis=0, tiled=True)  25.5 us
    all_to_all x1, waiting for transfers between devices, local(): lax.all_to_all(send_cot, 'expert', split_axis=0, concat_axis=0, tiled=True)  24.1 us
    all_to_all x1, starting transfers between devices, local(): lax.all_to_all(per_expert.reshape(n_experts, 1), 'expert', split_axis=0,...  22.8 us
    while x42, local copies, waits for them, and re-layouts  14.8 us
    dot_general x7, matrix products, weight_step(): lax.dot_general(grad_part, in_blk, contract_dims, preferred_element_type=...  11.4 us
  transfers between devices with their start and end apart: 5, of which 4 were waited for; matrix products, arithmetic and copies ran while one was open for 8% of the time, Pallas kernels for 0%

commit v1 on v0

v1 whole, which is shorter than its diff:
```python
import functools

import jax
import jax.numpy as jnp
from jax import lax
from jax.experimental import pallas as pl
from jax.experimental.pallas import tpu as pltpu
from jax.sharding import PartitionSpec as P

MESH = pl.DeviceIdType.MESH
EPS = 1e-05
CAP = 5
LANES = 128
NX = 4
CORES = 2
BF = jnp.bfloat16
F32 = jnp.float32


def ones_where(cond):
    return jnp.where(cond, 1.0, 0.0).astype(BF)


def fdot(a, b):
    return jnp.dot(a, b, preferred_element_type=F32)


def route_rows(shape, row_dim):
    r8 = lax.broadcasted_iota(jnp.int32, shape, row_dim)
    r5 = lax.broadcasted_iota(jnp.int32, shape, 1 - row_dim)
    base = lax.shift_right_logical(r8, 3) * CAP
    i = lax.bitwise_and(r8, 7)
    x_mask = jnp.where(i < CAP, base + i, -1) == r5
    c_mask = jnp.where(i >= CAP, base + i - CAP, -1) == r5
    f_row = base + 3 + lax.shift_right_logical(i, 2)
    g = lax.bitwise_and(i, 3)
    folds = [jnp.where(g == k, f_row, -1) == r5 for k in range(4)]
    return ones_where(x_mask), ones_where(c_mask), [ones_where(f) for f in folds]


def to_col(row, eye):
    return jnp.sum(jnp.where(eye, row, 0.0), axis=1, keepdims=True)


def kernel(
    cfg, tok_ref, gain_ref, routes_ref, gates_ref, win_ref, wout_ref, og_ref,
    mixed_ref, gg_ref, tg_ref, gin_ref, gout_ref,
    win, wout, send, recv, rsend, rrecv, rhs1, rhs2, std_ref,
    m1, m2, b1, b2, xs, cs, act, hg, gbuf, xbuf, sbuf, rbuf,
    w_sem, send_sem, recv_sem, rsend_sem, rrecv_sem, xs_sem, xr_sem, ss_sem, sr_sem,
):
    nz, ny, nch = cfg
    n_exp = NX * nz
    oc = n_exp // nch
    rows8, rows5 = oc * 8, oc * CAP
    frames, dim = tok_ref.shape
    ngrp = dim // LANES
    hid = win.shape[0]
    share = hid // (ny * CORES)
    half = ny // 2

    d = lax.axis_index("dp")
    e = lax.axis_index("expert")
    y, c = lax.div(d, CORES), lax.rem(d, CORES)
    x, z = lax.div(e, nz), lax.rem(e, nz)
    up = lax.rem(y + 1, ny) * CORES + c
    down = lax.rem(y + ny - 1, ny) * CORES + c
    mate = y * CORES + (1 - c)

    def offsets(o):
        p, xp = lax.div(o, NX), lax.rem(o, NX)
        odd = lax.rem(p, 2)
        dz = odd * lax.div(nz - 1 - p, 2) + (1 - odd) * lax.rem(nz // 2 + lax.div(p, 2), nz)
        return NX - 1 - xp, dz

    def peer_to(o):
        dx, dz = offsets(o)
        return (d, lax.rem(x + dx, NX) * nz + lax.rem(z + dz, nz))

    def peer_from(o):
        dx, dz = offsets(o)
        return (d, lax.rem(x + NX - dx, NX) * nz + lax.rem(z + nz - dz, nz))

    barrier = pltpu.get_barrier_semaphore()

    def greet(o, carry):
        pl.semaphore_signal(barrier, inc=1, device_id=peer_to(o), device_id_type=MESH)
        return carry

    lax.fori_loop(0, n_exp - 1, greet, 0)
    for other in (up, down, mate):
        pl.semaphore_signal(barrier, inc=1, device_id=(other, e), device_id_type=MESH)

    w_copies = [
        pltpu.make_async_copy(win_ref.at[0], win, w_sem.at[0]),
        pltpu.make_async_copy(wout_ref.at[0], wout, w_sem.at[1]),
    ]
    for copy in w_copies:
        copy.start()

    values = tok_ref[...].astype(F32)
    centered = values - jnp.mean(values, axis=1, keepdims=True)
    inv_std = lax.rsqrt(jnp.mean(centered * centered, axis=1, keepdims=True) + EPS)
    standard = centered * inv_std
    std_ref[...] = standard
    gain = gain_ref[...]
    rhs1[0:frames, :] = (standard * gain).astype(BF)

    f_row = lax.broadcasted_iota(jnp.int32, (frames, frames), 0)
    f_col = lax.broadcasted_iota(jnp.int32, (frames, frames), 1)
    eye = f_row == f_col
    og = og_ref[...].astype(F32)
    gates = [to_col(gates_ref[k : k + 1, :], eye) for k in range(2)]
    for k in range(2):
        scaled = (gates[k] * og).astype(BF)
        rhs1[frames * (k + 1) : frames * (k + 2), :] = scaled
        for g in range(ngrp):
            at = (k * ngrp + g) * frames
            rhs2[at : at + frames, :] = scaled[:, g * LANES : (g + 1) * LANES]

    rels, hots = [], []
    e_iota = lax.broadcasted_iota(jnp.int32, (n_exp, frames), 0)
    for k in range(2):
        r = routes_ref[k : k + 1, :]
        dx = lax.bitwise_and(lax.shift_right_logical(r, nz.bit_length() - 1) - x, NX - 1)
        dz = lax.bitwise_and(r - z, nz - 1)
        p = jnp.where(dz < nz // 2, nz - 1 - 2 * dz, 2 * dz - nz)
        rel = p * NX + (NX - 1 - dx)
        rels.append(rel)
        hots.append(jnp.where(e_iota == rel, 1.0, 0.0))
    before = fdot((hots[0] + hots[1]).astype(BF), ones_where(f_row < f_col))
    dest_a, dest_b, dest_f = [], [], []
    for k in range(2):
        slot = jnp.sum(hots[k] * before, axis=0, keepdims=True)
        base = rels[k].astype(F32) * 8.0
        dest_a.append(base + slot)
        dest_b.append(jnp.where(slot < 3.0, base + 5.0 + slot, -1.0))
        dest_f.append(jnp.where(slot >= 3.0, base + (slot - 3.0) * 4.0, -100.0))

    pl.semaphore_wait(barrier, n_exp + 2)

    def dispatch(o, q):
        return pltpu.make_async_remote_copy(
            src_ref=send.at[o], dst_ref=recv.at[o], send_sem=send_sem, recv_sem=recv_sem.at[q],
            device_id=peer_to(o), device_id_type=MESH,
        )

    def give_back(o, q):
        return pltpu.make_async_remote_copy(
            src_ref=rsend.at[o], dst_ref=rrecv.at[o], send_sem=rsend_sem, recv_sem=rrecv_sem.at[q],
            device_id=peer_from(o), device_id_type=MESH,
        )

    own = n_exp - 1

    def send_chunk(q, carry):
        rid = (lax.broadcasted_iota(jnp.int32, (rows8, frames), 0) + q * rows8).astype(F32)
        a = ones_where((rid == dest_a[0]) | (rid == dest_a[1]))
        lhs1 = jnp.concatenate([a] + [ones_where(rid == dest_b[k]) for k in range(2)], axis=1)
        lhs2 = jnp.concatenate(
            [ones_where(rid == dest_f[k] + float(g)) for k in range(2) for g in range(ngrp)], axis=1
        )
        first = q * oc
        send[pl.ds(first, oc), :, 0:dim] = fdot(lhs1, rhs1[...]).reshape(oc, 8, dim).astype(BF)
        send[pl.ds(first, oc), :, dim : dim + LANES] = (
            fdot(lhs2, rhs2[...]).reshape(oc, 8, LANES).astype(BF)
        )

        def start(i, carry):
            dispatch(first + i, q).start()
            return carry

        lax.fori_loop(0, jnp.where(q == nch - 1, oc - 1, oc), start, 0)
        return carry

    lax.fori_loop(0, nch, send_chunk, 0)
    own_copy = pltpu.make_async_copy(send.at[own], recv.at[own], recv_sem.at[nch - 1])
    own_copy.start()

    xm, cm, fm = route_rows((rows5, rows8), 1)
    m1[0:rows5, :] = xm
    m1[rows5 : 2 * rows5, :] = cm
    for g in range(ngrp):
        m2[g * rows5 : (g + 1) * rows5, :] = fm[g]
    xt, ct, ft = route_rows((rows8, rows5), 0)
    b1[...] = jnp.concatenate([xt, ct], axis=1)
    b2[...] = jnp.concatenate(ft, axis=1)

    for copy in w_copies:
        copy.wait()

    n_blk = 4
    blk = hid // n_blk
    nt = (((1,), (1,)), ((), ()))

    def expert_chunk(q, carry):
        first = q * oc
        row = pl.multiple_of(q * rows5, rows5)
        pltpu.make_async_copy(
            recv.at[pl.ds(first, oc)], recv.at[pl.ds(first, oc)], recv_sem.at[q]
        ).wait()
        msg = recv[pl.ds(first, oc)].astype(F32).reshape(rows8, dim + LANES).astype(BF)
        both = fdot(m1[...], msg[:, 0:dim])
        folded = fdot(m2[...], msg[:, dim : dim + LANES])
        x_in = both[0:rows5].astype(BF)
        fold_cat = jnp.concatenate(
            [folded[g * rows5 : (g + 1) * rows5] for g in range(ngrp)], axis=1
        )
        cot = (both[rows5 : 2 * rows5] + fold_cat).astype(BF)
        xs[pl.ds(row, rows5), :] = x_in
        cs[pl.ds(row, rows5), :] = cot
        out = jnp.zeros((rows5, dim), F32)
        ingrad = jnp.zeros((rows5, dim), F32)
        for b in range(n_blk):
            at = slice(b * blk, (b + 1) * blk)
            pre = lax.dot_general(x_in, win[at, :], nt, preferred_element_type=F32)
            back = lax.dot_general(cot, wout[at, :], nt, preferred_element_type=F32)
            sg = 0.5 * jnp.tanh(0.5 * pre) + 0.5
            act_b = (pre * sg).astype(BF)
            hg_b = (back * (sg * (1.0 + pre * (1.0 - sg)))).astype(BF)
            act[pl.ds(row, rows5), at] = act_b
            hg[pl.ds(row, rows5), at] = hg_b
            out = out + fdot(act_b, wout[at, :])
            ingrad = ingrad + fdot(hg_b, win[at, :])
        out_h, in_h = out.astype(BF), ingrad.astype(BF)
        rmain = fdot(b1[...], jnp.concatenate([out_h, in_h], axis=0))
        stack = jnp.concatenate(
            [in_h[:, g * LANES : (g + 1) * LANES] for g in range(ngrp)], axis=0
        )
        rfold = fdot(b2[...], stack)
        rsend[pl.ds(first, oc), :, 0:dim] = rmain.reshape(oc, 8, dim).astype(BF)
        rsend[pl.ds(first, oc), :, dim : dim + LANES] = rfold.reshape(oc, 8, LANES).astype(BF)

        def start(i, carry):
            give_back(first + i, q).start()
            return carry

        lax.fori_loop(0, jnp.where(q == nch - 1, oc - 1, oc), start, 0)
        return carry

    lax.fori_loop(0, nch, expert_chunk, 0)
    own_back = pltpu.make_async_copy(rsend.at[own], rrecv.at[own], rrecv_sem.at[nch - 1])
    own_back.start()

    tn = (((0,), (0,)), ((), ()))

    def exchange(j):
        return pltpu.make_async_remote_copy(
            src_ref=gbuf.at[j, :, pl.ds((1 - c) * share, share), :], dst_ref=xbuf.at[j],
            send_sem=xs_sem.at[j], recv_sem=xr_sem.at[j], device_id=(mate, e), device_id_type=MESH,
        )

    def grads(j):
        shift = half - (j + 1) // 2 if j % 2 else (half + j // 2) % ny
        at = pl.multiple_of(lax.rem(y + shift, ny) * (CORES * share), CORES * share)
        cols = pl.ds(at, CORES * share)
        gbuf[j, 0] = lax.dot_general(hg[:, cols], xs[...], tn, preferred_element_type=F32).astype(BF)
        gbuf[j, 1] = lax.dot_general(act[:, cols], cs[...], tn, preferred_element_type=F32).astype(BF)
        exchange(j).start()

    def term(j, part):
        mine = gbuf[j, part, pl.ds(pl.multiple_of(c * share, share), share), :].astype(F32)
        return mine + xbuf[j, part].astype(F32)

    def hop(way, step, part):
        return pltpu.make_async_remote_copy(
            src_ref=sbuf.at[way, step, part], dst_ref=rbuf.at[way, step, part],
            send_sem=ss_sem.at[way, step, part], recv_sem=sr_sem.at[way, step, part],
            device_id=((up, down)[way], e), device_id_type=MESH,
        )

    def parts_of(way, step):
        return ((way,) if step == 0 else (1 - way, way))

    hops = []
    grads(0)
    for step in range(half):
        js = (0,) if step == 0 else (2 * step - 1, 2 * step)
        ahead = [j for j in (2 * step + 1, 2 * step + 2) if j < ny]
        for j in ahead:
            grads(j)
        for j in js:
            exchange(j).wait_recv()
        order = (0, 1) if step == 1 or step == 0 else (0, 1)
        for i in order:
            for way in range(2):
                parts = parts_of(way, step)
                if i >= len(parts):
                    continue
                part = parts[i]
                j = js[way] if step else 0
                total = term(j, part)
                if step and part in parts_of(way, step - 1):
                    hop(way, step - 1, part).wait_recv()
                    total = total + rbuf[way, step - 1, part].astype(F32)
                sbuf[way, step, part] = total.astype(BF)
                copy = hop(way, step, part)
                copy.start()
                hops.append(copy)

    lane_id = lax.broadcasted_iota(jnp.int32, (frames, n_exp * 8), 1).astype(F32)
    cols_a = [to_col(dest_a[k], eye) for k in range(2)]
    cols_b = [to_col(dest_b[k], eye) for k in range(2)]
    cols_f = [to_col(dest_f[k], eye) for k in range(2)]
    pick_a = [ones_where(lane_id == cols_a[k]) for k in range(2)]
    pick_b = ones_where((lane_id == cols_b[0]) | (lane_id == cols_b[1]))
    pick_f = [
        ones_where((lane_id == cols_f[0] + float(g)) | (lane_id == cols_f[1] + float(g)))
        for g in range(ngrp)
    ]
    for q in range(nch):
        pltpu.make_async_copy(
            rrecv.at[pl.ds(q * oc, oc)], rrecv.at[pl.ds(q * oc, oc)], rrecv_sem.at[q]
        ).wait()
    msg = rrecv[...].astype(F32).reshape(n_exp * 8, dim + LANES).astype(BF)
    main, fold = msg[:, 0:dim], msg[:, dim : dim + LANES]
    og = og_ref[...].astype(F32)
    y_rows = [fdot(pick_a[k], main) for k in range(2)]
    mixed_ref[...] = (gates[0] * y_rows[0] + gates[1] * y_rows[1]).astype(BF)
    for k in range(2):
        dots = jnp.sum(og * y_rows[k], axis=1, keepdims=True)
        gg_ref[k : k + 1, :] = jnp.sum(jnp.where(eye, dots, 0.0), axis=0, keepdims=True)
    du = fdot(pick_b, main) + jnp.concatenate([fdot(pick_f[g], fold) for g in range(ngrp)], axis=1)
    norm_grad = du * gain
    standard = std_ref[...]
    tg_ref[...] = (
        inv_std
        * (
            norm_grad
            - jnp.mean(norm_grad, axis=1, keepdims=True)
            - standard * jnp.mean(norm_grad * standard, axis=1, keepdims=True)
        )
    ).astype(BF)

    last = half - 1
    exchange(ny - 1).wait_recv()
    for part, out_ref in ((0, gin_ref), (1, gout_ref)):
        total = term(ny - 1, part)
        for way in range(2):
            if part in parts_of(way, last):
                hop(way, last, part).wait_recv()
                total = total + rbuf[way, last, part].astype(F32)
        out_ref[0] = total

    pltpu.make_async_copy(send.at[pl.ds(0, own)], send.at[pl.ds(0, own)], send_sem).wait()
    pltpu.make_async_copy(rsend.at[pl.ds(0, own)], rsend.at[pl.ds(0, own)], rsend_sem).wait()
    for j in range(ny):
        exchange(j).wait_send()
    for copy in hops:
        copy.wait_send()


def local(nz, ny, nch, tokens, norm_gain, routes, gate_weights, weight_in, weight_out, out_grad):
    frames, dim = tokens.shape
    hid = weight_in.shape[1]
    n_exp = NX * nz
    oc = n_exp // nch
    share = hid // (ny * CORES)
    half = ny // 2
    ngrp = dim // LANES
    total = n_exp * CAP
    msgs = pltpu.VMEM((n_exp, 8, dim + LANES), BF)
    dma = pltpu.SemaphoreType.DMA
    vmem = pl.BlockSpec(memory_space=pltpu.VMEM)
    hbm = pl.BlockSpec(memory_space=pl.ANY)
    mixed, gate_grad, token_grad, gin, gout = pl.pallas_call(
        functools.partial(kernel, (nz, ny, nch)),
        out_shape=(
            jax.ShapeDtypeStruct((frames, dim), BF),
            jax.ShapeDtypeStruct((2, frames), F32),
            jax.ShapeDtypeStruct((frames, dim), BF),
            jax.ShapeDtypeStruct((1, share, dim), F32),
            jax.ShapeDtypeStruct((1, share, dim), F32),
        ),
        in_specs=[vmem, vmem, vmem, vmem, hbm, hbm, vmem],
        out_specs=(vmem,) * 5,
        scratch_shapes=[
            pltpu.VMEM((hid, dim), BF),
            pltpu.VMEM((hid, dim), BF),
            msgs, msgs, msgs, msgs,
            pltpu.VMEM((3 * frames, dim), BF),
            pltpu.VMEM((2 * ngrp * frames, LANES), BF),
            pltpu.VMEM((frames, dim), F32),
            pltpu.VMEM((2 * oc * CAP, oc * 8), BF),
            pltpu.VMEM((ngrp * oc * CAP, oc * 8), BF),
            pltpu.VMEM((oc * 8, 2 * oc * CAP), BF),
            pltpu.VMEM((oc * 8, ngrp * oc * CAP), BF),
            pltpu.VMEM((total, dim), BF),
            pltpu.VMEM((total, dim), BF),
            pltpu.VMEM((total, hid), BF),
            pltpu.VMEM((total, hid), BF),
            pltpu.VMEM((ny, 2, CORES * share, dim), BF),
            pltpu.VMEM((ny, 2, share, dim), BF),
            pltpu.VMEM((2, half, 2, share, dim), BF),
            pltpu.VMEM((2, half, 2, share, dim), BF),
            dma((2,)), dma, dma((nch,)), dma, dma((nch,)),
            dma((ny,)), dma((ny,)), dma((2, half, 2)), dma((2, half, 2)),
        ],
        compiler_params=pltpu.CompilerParams(
            collective_id=0, has_side_effects=True, vmem_limit_bytes=52 * 1024 * 1024
        ),
    )(
        tokens, norm_gain.reshape(1, dim), routes.T, gate_weights.T, weight_in, weight_out, out_grad
    )
    return mixed, gate_grad.T, token_grad, gin, gout


def solution(mesh):
    nz = mesh.shape["expert"] // NX
    ny = mesh.shape["dp"] // CORES
    frames = P(("dp", "expert"), None)
    weights = P("expert", None, None)
    return jax.shard_map(
        functools.partial(local, nz, ny, 4),
        mesh=mesh,
        in_specs=(frames, P(), frames, frames, weights, weights, frames),
        out_specs=(frames, frames, frames, P("expert", "dp", None), P("expert", "dp", None)),
        check_vma=False,
    )
```

time: 362 us -> 95.4 us (0.26)
  Pallas kernels: 0 us -> 87.4 us
  waiting for transfers between devices: 82.8 us -> 0 us
  blocking collectives: 75.2 us -> 0 us
  matrix products: 73.1 us -> 0 us
  starting transfers between devices: 49.4 us -> 0 us
  local copies, waits for them, and re-layouts: 44.1 us -> 7.12 us
  other arithmetic: 18.9 us -> 0 us
  between operations: 15.1 us -> 0.66 us
    pallas_call x0 -> x1, Pallas kernels: none -> 87.4 us  [local(): pl.pallas_call(functools.partial(kernel, (nz, ny, nch)), out_shape=(jax.S...]
    all_to_all x4 -> x0, waiting for transfers between devices: 82.8 us -> none  [the longest x1 26.8 us: local(): lax.all_to_all(back_y, 'expert', split_axis=0, concat_axis=0, tiled=True)]
    all_to_all x1 -> x0, blocking collectives: 75.2 us -> none  [local(): lax.all_to_all(back_du, 'expert', split_axis=0, concat_axis=0, tiled=True)]
    dot_general x43 -> x0, matrix products: 73.1 us -> none  [the longest x7 35.7 us: weight_step(): lax.dot_general(act_part, cot_blk, contract_dims, preferred_element_type=...]
    all_to_all x4 -> x0, starting transfers between devices: 49.3 us -> none  [the longest x1 22.8 us: local(): lax.all_to_all(per_expert.reshape(n_experts, 1), 'expert', split_axis=0,...]
    while x42 -> x0, local copies, waits for them, and re-layouts: 14.8 us -> none
    another operation x7 -> x0, local copies, waits for them, and re-layouts: 7.6 us -> none
    gather x6 -> x0, local copies, waits for them, and re-layouts: 6.61 us -> none  [the longest x2 2.15 us: local(): expert_out[pick_row]]
  transfers between devices with their start and end apart: 5 -> 0, of which waited for: 4 -> 0; matrix products, arithmetic and copies ran while one was open for 8% -> 0% of each run, Pallas kernels for 0% -> 0%
where the time goes in v1:
time: 95.4 us; the launch traced here: 95.2 us
  Pallas kernels  87.4 us (92%)
  local copies, waits for them, and re-layouts  7.12 us (7%)
    pallas_call x1, Pallas kernels, local(): pl.pallas_call(functools.partial(kernel, (nz, ny, nch)), out_shape=(jax.S...  87.4 us
    unnamed x15, local copies, waits for them, and re-layouts  7.12 us

profile of v1, /device:TPU:1, one launch (start us, length us, event | category | flops | bytes accessed | tf_op | source)
XLA Modules:
  0.0 95.2 jit_solution(1071168826005525851)
XLA Ops:
  0.6 0.0 copy-start
  0.6 0.9 copy-done
  1.5 0.0 copy-start.1
  1.5 0.9 copy-done.1
  2.4 0.0 copy-start.2
  2.4 0.7 copy-done.2
  3.1 0.0 copy-start.3
  3.1 0.7 copy-done.3
  3.8 0.0 copy-start.4
  3.8 0.7 copy-done.4
  4.5 87.4 %shard_map.110 = (bf16[128,512]{1,0:T(8,128)(2,1)S(1)}, f32[2,128]{1,0:T(2,128)S(1)}, bf16[128,512]{1,0:T(8,128)(2,1)S(1)}, f32[1,128,512]{2,1,0:T(8,128)S(1)}, f32[1,128,512]{2,1,0:T(8,128)S(1)}) custom-call(bf16[128,512]{1,0:T(8,128)(2,1)S(1)} %copy-done, f32[1,512]{1,0:T(1,128)S(1)} %bitcast.4, s32[2,128]{1,0:T(2,128)S(1)} %bitcast.5, ...), custom_call_target="tpu_custom_call" | custom-call | tf_op jit(solution)/shard_map/pallas_call | solution.py:366
  91.9 0.7 copy.17
  92.5 0.6 copy.18
  93.1 0.7 copy.19
  93.7 0.7 copy.20
  94.5 0.7 copy.21
Async XLA Ops:
  0.6 0.9 copy-start
  1.5 0.9 copy-start.1
  2.4 0.7 copy-start.2
  3.1 0.7 copy-start.3
  3.8 0.7 copy-start.4

commit v2 on v1

--- a/solution.py
+++ b/solution.py
@@ -13,6 +13,8 @@
 LANES = 128
 NX = 4
 CORES = 2
+DELAY = 2
+VMEM_BYTES = 60 * 1024 * 1024
 BF = jnp.bfloat16
 F32 = jnp.float32
 
@@ -43,11 +45,13 @@
 
 
 def kernel(
-    cfg, tok_ref, gain_ref, routes_ref, gates_ref, win_ref, wout_ref, og_ref,
+    cfg, tok_hbm, gain_hbm, routes_hbm, gates_hbm, win_ref, wout_ref, og_hbm,
+    mixed_hbm, gg_hbm, tg_hbm, gin_hbm, gout_hbm,
     mixed_ref, gg_ref, tg_ref, gin_ref, gout_ref,
+    tok_ref, gain_ref, routes_ref, gates_ref, og_ref,
     win, wout, send, recv, rsend, rrecv, rhs1, rhs2, std_ref,
     m1, m2, b1, b2, xs, cs, act, hg, gbuf, xbuf, sbuf, rbuf,
-    w_sem, send_sem, recv_sem, rsend_sem, rrecv_sem, xs_sem, xr_sem, ss_sem, sr_sem,
+    in_sem, out_sem, w_sem, send_sem, recv_sem, rsend_sem, rrecv_sem, xs_sem, xr_sem, ss_sem, sr_sem,
 ):
     nz, ny, nch = cfg
     n_exp = NX * nz
@@ -81,6 +85,21 @@
         dx, dz = offsets(o)
         return (d, lax.rem(x + NX - dx, NX) * nz + lax.rem(z + nz - dz, nz))
 
+    in_copies = [
+        pltpu.make_async_copy(src, dst, in_sem.at[i])
+        for i, (src, dst) in enumerate(
+            (
+                (routes_hbm, routes_ref),
+                (gates_hbm, gates_ref),
+                (tok_hbm, tok_ref),
+                (gain_hbm, gain_ref),
+                (og_hbm, og_ref),
+            )
+        )
+    ]
+    for copy in in_copies:
+        copy.start()
+
     barrier = pltpu.get_barrier_semaphore()
 
     def greet(o, carry):
@@ -98,6 +117,8 @@
     for copy in w_copies:
         copy.start()
 
+    for copy in in_copies:
+        copy.wait()
     values = tok_ref[...].astype(F32)
     centered = values - jnp.mean(values, axis=1, keepdims=True)
     inv_std = lax.rsqrt(jnp.mean(centered * centered, axis=1, keepdims=True) + EPS)
@@ -193,12 +214,21 @@
     blk = hid // n_blk
     nt = (((1,), (1,)), ((), ()))
 
+    def return_chunk(q):
+        def start(i, carry):
+            give_back(q * oc + i, q).start()
+            return carry
+
+        lax.fori_loop(0, jnp.where(q == nch - 1, oc - 1, oc), start, 0)
+
     def expert_chunk(q, carry):
         first = q * oc
         row = pl.multiple_of(q * rows5, rows5)
         pltpu.make_async_copy(
             recv.at[pl.ds(first, oc)], recv.at[pl.ds(first, oc)], recv_sem.at[q]
         ).wait()
+        if DELAY:
+            pl.when(q >= DELAY)(lambda: return_chunk(q - DELAY))
         msg = recv[pl.ds(first, oc)].astype(F32).reshape(rows8, dim + LANES).astype(BF)
         both = fdot(m1[...], msg[:, 0:dim])
         folded = fdot(m2[...], msg[:, dim : dim + LANES])
@@ -231,14 +261,11 @@
         rsend[pl.ds(first, oc), :, 0:dim] = rmain.reshape(oc, 8, dim).astype(BF)
         rsend[pl.ds(first, oc), :, dim : dim + LANES] = rfold.reshape(oc, 8, LANES).astype(BF)
 
-        def start(i, carry):
-            give_back(first + i, q).start()
-            return carry
-
-        lax.fori_loop(0, jnp.where(q == nch - 1, oc - 1, oc), start, 0)
         return carry
 
     lax.fori_loop(0, nch, expert_chunk, 0)
+    if DELAY:
+        lax.fori_loop(nch - DELAY, nch, lambda q, carry: (return_chunk(q), carry)[1], 0)
     own_back = pltpu.make_async_copy(rsend.at[own], rrecv.at[own], rrecv_sem.at[nch - 1])
     own_back.start()
 
@@ -308,29 +335,18 @@
         ones_where((lane_id == cols_f[0] + float(g)) | (lane_id == cols_f[1] + float(g)))
         for g in range(ngrp)
     ]
-    for q in range(nch):
-        pltpu.make_async_copy(
-            rrecv.at[pl.ds(q * oc, oc)], rrecv.at[pl.ds(q * oc, oc)], rrecv_sem.at[q]
-        ).wait()
-    msg = rrecv[...].astype(F32).reshape(n_exp * 8, dim + LANES).astype(BF)
-    main, fold = msg[:, 0:dim], msg[:, dim : dim + LANES]
-    og = og_ref[...].astype(F32)
-    y_rows = [fdot(pick_a[k], main) for k in range(2)]
-    mixed_ref[...] = (gates[0] * y_rows[0] + gates[1] * y_rows[1]).astype(BF)
-    for k in range(2):
-        dots = jnp.sum(og * y_rows[k], axis=1, keepdims=True)
-        gg_ref[k : k + 1, :] = jnp.sum(jnp.where(eye, dots, 0.0), axis=0, keepdims=True)
-    du = fdot(pick_b, main) + jnp.concatenate([fdot(pick_f[g], fold) for g in range(ngrp)], axis=1)
-    norm_grad = du * gain
-    standard = std_ref[...]
-    tg_ref[...] = (
-        inv_std
-        * (
-            norm_grad
-            - jnp.mean(norm_grad, axis=1, keepdims=True)
-            - standard * jnp.mean(norm_grad * standard, axis=1, keepdims=True)
-        )
-    ).astype(BF)
+    outs = [
+        pltpu.make_async_copy(src, dst, out_sem.at[i])
+        for i, (src, dst) in enumerate(
+            (
+                (mixed_ref, mixed_hbm),
+                (gg_ref, gg_hbm),
+                (tg_ref, tg_hbm),
+                (gin_ref, gin_hbm),
+                (gout_ref, gout_hbm),
+            )
+        )
+    ]
 
     last = half - 1
     exchange(ny - 1).wait_recv()
@@ -341,6 +357,38 @@
                 hop(way, last, part).wait_recv()
                 total = total + rbuf[way, last, part].astype(F32)
         out_ref[0] = total
+        outs[3 + part].start()
+
+    y_rows = [jnp.zeros((frames, dim), F32) for k in range(2)]
+    du = jnp.zeros((frames, dim), F32)
+    for q in range(nch):
+        pltpu.make_async_copy(
+            rrecv.at[pl.ds(q * oc, oc)], rrecv.at[pl.ds(q * oc, oc)], rrecv_sem.at[q]
+        ).wait()
+        msg = rrecv[q * oc : (q + 1) * oc].astype(F32).reshape(rows8, dim + LANES).astype(BF)
+        main, fold = msg[:, 0:dim], msg[:, dim : dim + LANES]
+        at = slice(q * rows8, (q + 1) * rows8)
+        y_rows = [y_rows[k] + fdot(pick_a[k][:, at], main) for k in range(2)]
+        folded = [fdot(pick_f[g][:, at], fold) for g in range(ngrp)]
+        du = du + fdot(pick_b[:, at], main) + jnp.concatenate(folded, axis=1)
+    og = og_ref[...].astype(F32)
+    mixed_ref[...] = (gates[0] * y_rows[0] + gates[1] * y_rows[1]).astype(BF)
+    for k in range(2):
+        dots = jnp.sum(og * y_rows[k], axis=1, keepdims=True)
+        gg_ref[k : k + 1, :] = jnp.sum(jnp.where(eye, dots, 0.0), axis=0, keepdims=True)
+    norm_grad = du * gain
+    standard = std_ref[...]
+    tg_ref[...] = (
+        inv_std
+        * (
+            norm_grad
+            - jnp.mean(norm_grad, axis=1, keepdims=True)
+            - standard * jnp.mean(norm_grad * standard, axis=1, keepdims=True)
+        )
+    ).astype(BF)
+
+    for i in range(3):
+        outs[i].start()
 
     pltpu.make_async_copy(send.at[pl.ds(0, own)], send.at[pl.ds(0, own)], send_sem).wait()
     pltpu.make_async_copy(rsend.at[pl.ds(0, own)], rsend.at[pl.ds(0, own)], rsend_sem).wait()
@@ -348,6 +396,30 @@
         exchange(j).wait_send()
     for copy in hops:
         copy.wait_send()
+    for copy in outs:
+        copy.wait()
+
+
+def store_kernel(*refs):
+    n = (len(refs) - 1) // 2
+    copies = [
+        pltpu.make_async_copy(refs[i], refs[n + i], refs[2 * n].at[i]) for i in range(n)
+    ]
+    for copy in copies:
+        copy.start()
+    for copy in copies:
+        copy.wait()
+
+
+def store(*arrays):
+    return pl.pallas_call(
+        store_kernel,
+        out_shape=tuple(jax.ShapeDtypeStruct(a.shape, a.dtype) for a in arrays),
+        in_specs=[pl.BlockSpec(memory_space=pltpu.VMEM)] * len(arrays),
+        out_specs=(pl.BlockSpec(memory_space=pltpu.HBM),) * len(arrays),
+        scratch_shapes=[pltpu.SemaphoreType.DMA((len(arrays),))],
+        compiler_params=pltpu.CompilerParams(vmem_limit_bytes=VMEM_BYTES),
+    )(*arrays)
 
 
 def local(nz, ny, nch, tokens, norm_gain, routes, gate_weights, weight_in, weight_out, out_grad):
@@ -361,8 +433,7 @@
     total = n_exp * CAP
     msgs = pltpu.VMEM((n_exp, 8, dim + LANES), BF)
     dma = pltpu.SemaphoreType.DMA
-    vmem = pl.BlockSpec(memory_space=pltpu.VMEM)
-    hbm = pl.BlockSpec(memory_space=pl.ANY)
+    hbm = pl.BlockSpec(memory_space=pltpu.HBM)
     mixed, gate_grad, token_grad, gin, gout = pl.pallas_call(
         functools.partial(kernel, (nz, ny, nch)),
         out_shape=(
@@ -372,9 +443,19 @@
             jax.ShapeDtypeStruct((1, share, dim), F32),
             jax.ShapeDtypeStruct((1, share, dim), F32),
         ),
-        in_specs=[vmem, vmem, vmem, vmem, hbm, hbm, vmem],
-        out_specs=(vmem,) * 5,
+        in_specs=[hbm] * 7,
+        out_specs=(hbm,) * 5,
         scratch_shapes=[
+            pltpu.VMEM((frames, dim), BF),
+            pltpu.VMEM((2, frames), F32),
+            pltpu.VMEM((frames, dim), BF),
+            pltpu.VMEM((1, share, dim), F32),
+            pltpu.VMEM((1, share, dim), F32),
+            pltpu.VMEM((frames, dim), BF),
+            pltpu.VMEM((1, dim), F32),
+            pltpu.VMEM((2, frames), jnp.int32),
+            pltpu.VMEM((2, frames), F32),
+            pltpu.VMEM((frames, dim), BF),
             pltpu.VMEM((hid, dim), BF),
             pltpu.VMEM((hid, dim), BF),
             msgs, msgs, msgs, msgs,
@@ -393,15 +474,16 @@
             pltpu.VMEM((ny, 2, share, dim), BF),
             pltpu.VMEM((2, half, 2, share, dim), BF),
             pltpu.VMEM((2, half, 2, share, dim), BF),
-            dma((2,)), dma, dma((nch,)), dma, dma((nch,)),
+            dma((5,)), dma((5,)), dma((2,)), dma, dma((nch,)), dma, dma((nch,)),
             dma((ny,)), dma((ny,)), dma((2, half, 2)), dma((2, half, 2)),
         ],
         compiler_params=pltpu.CompilerParams(
-            collective_id=0, has_side_effects=True, vmem_limit_bytes=52 * 1024 * 1024
+            collective_id=0, has_side_effects=True, vmem_limit_bytes=VMEM_BYTES
         ),
     )(
         tokens, norm_gain.reshape(1, dim), routes.T, gate_weights.T, weight_in, weight_out, out_grad
     )
+    mixed, gate_grad, token_grad, gin, gout = store(mixed, gate_grad, token_grad, gin, gout)
     return mixed, gate_grad.T, token_grad, gin, gout
 
 

time: 95.4 us -> 89.9 us (0.942)
  local copies, waits for them, and re-layouts: 7.12 us -> 0 us
  Pallas kernels: 87.4 us -> 89.1 us
    unnamed x15 -> x0, local copies, waits for them, and re-layouts: 7.12 us -> none
    pallas_call x0 -> x1, Pallas kernels: none -> 2.08 us  [store(): pl.pallas_call(store_kernel, out_shape=tuple((jax.ShapeDtypeStruct(a.shap...]
where the time goes in v2:
time: 89.9 us; the launch traced here: 89.8 us
  Pallas kernels  89.1 us (99%)
    pallas_call x1, Pallas kernels, local(): pl.pallas_call(functools.partial(kernel, (nz, ny, nch)), out_shape=(jax.S...  87 us
    pallas_call x1, Pallas kernels, store(): pl.pallas_call(store_kernel, out_shape=tuple((jax.ShapeDtypeStruct(a.shap...  2.08 us

profile of v2, /device:TPU:1, one launch (start us, length us, event | category | flops | bytes accessed | tf_op | source)
XLA Modules:
  0.0 89.8 jit_solution(6439387248784359153)
XLA Ops:
  0.6 87.0 %shard_map.110 = (bf16[128,512]{1,0:T(8,128)(2,1)}, f32[2,128]{1,0:T(2,128)}, bf16[128,512]{1,0:T(8,128)(2,1)}, f32[1,128,512]{2,1,0:T(8,128)}, f32[1,128,512]{2,1,0:T(8,128)}) custom-call(bf16[128,512]{1,0:T(8,128)(2,1)} %tok_hbm.1, f32[1,512]{1,0:T(1,128)} %bitcast.4, s32[2,128]{1,0:T(2,128)} %bitcast.5, f32[2,128]{1,0:T(2,128)} %bitcast.6, ...), custom_call_target="tpu_custom_call" | custom-call | tf_op jit(solution)/shard_map/pallas_call | solution.py:437
  87.7 2.1 %shard_map.111 = (bf16[128,512]{1,0:T(8,128)(2,1)}, f32[2,128]{1,0:T(2,128)}, bf16[128,512]{1,0:T(8,128)(2,1)}, f32[1,128,512]{2,1,0:T(8,128)}, f32[1,128,512]{2,1,0:T(8,128)}) custom-call(bf16[128,512]{1,0:T(8,128)(2,1)} %get-tuple-element.15.refs_0_, f32[2,128]{1,0:T(2,128)} %get-tuple-element.16.refs_1_, bf16[128,512]{1,0:T(8,128)(2,1)} %get-tuple-element.17.refs_2_, ...), custom_call_target="tpu_custom_call" | custom-call | tf_op jit(solution)/shard_map/pallas_call | solution.py:415

commit v3 on v2

--- a/solution.py
+++ b/solution.py
@@ -71,19 +71,35 @@
     down = lax.rem(y + ny - 1, ny) * CORES + c
     mate = y * CORES + (1 - c)
 
-    def offsets(o):
-        p, xp = lax.div(o, NX), lax.rem(o, NX)
+    def column(p):
         odd = lax.rem(p, 2)
-        dz = odd * lax.div(nz - 1 - p, 2) + (1 - odd) * lax.rem(nz // 2 + lax.div(p, 2), nz)
-        return NX - 1 - xp, dz
-
-    def peer_to(o):
-        dx, dz = offsets(o)
-        return (d, lax.rem(x + dx, NX) * nz + lax.rem(z + dz, nz))
-
-    def peer_from(o):
-        dx, dz = offsets(o)
-        return (d, lax.rem(x + NX - dx, NX) * nz + lax.rem(z + nz - dz, nz))
+        return odd * lax.div(nz - 1 - p, 2) + (1 - odd) * lax.rem(nz // 2 + lax.div(p, 2), nz)
+
+    to_x = [lax.rem(x + NX - 1 - xp, NX) * nz for xp in range(NX)]
+    from_x = [lax.rem(x + 1 + xp, NX) * nz for xp in range(NX)]
+
+    def to_z(p):
+        return lax.rem(z + column(p), nz)
+
+    def from_z(p):
+        return lax.rem(z + nz - column(p), nz)
+
+    def each_peer(first, last, act):
+        def columns(p, carry):
+            for xp in range(NX):
+                act(p, xp)
+            return carry
+
+        lax.fori_loop(first, jnp.minimum(last, nz - 1), columns, 0)
+
+        def rest():
+            for xp in range(NX - 1):
+                act(nz - 1, xp)
+
+        if isinstance(last, int):
+            rest()
+        else:
+            pl.when(last == nz)(rest)
 
     in_copies = [
         pltpu.make_async_copy(src, dst, in_sem.at[i])
@@ -102,11 +118,12 @@
 
     barrier = pltpu.get_barrier_semaphore()
 
-    def greet(o, carry):
-        pl.semaphore_signal(barrier, inc=1, device_id=peer_to(o), device_id_type=MESH)
-        return carry
-
-    lax.fori_loop(0, n_exp - 1, greet, 0)
+    def greet(p, xp):
+        pl.semaphore_signal(
+            barrier, inc=1, device_id=(d, to_x[xp] + to_z(p)), device_id_type=MESH
+        )
+
+    each_peer(0, nz, greet)
     for other in (up, down, mate):
         pl.semaphore_signal(barrier, inc=1, device_id=(other, e), device_id_type=MESH)
 
@@ -160,18 +177,21 @@
 
     pl.semaphore_wait(barrier, n_exp + 2)
 
-    def dispatch(o, q):
-        return pltpu.make_async_remote_copy(
+    def dispatch(q, p, xp):
+        o = p * NX + xp
+        pltpu.make_async_remote_copy(
             src_ref=send.at[o], dst_ref=recv.at[o], send_sem=send_sem, recv_sem=recv_sem.at[q],
-            device_id=peer_to(o), device_id_type=MESH,
-        )
-
-    def give_back(o, q):
-        return pltpu.make_async_remote_copy(
+            device_id=(d, to_x[xp] + to_z(p)), device_id_type=MESH,
+        ).start()
+
+    def give_back(q, p, xp):
+        o = p * NX + xp
+        pltpu.make_async_remote_copy(
             src_ref=rsend.at[o], dst_ref=rrecv.at[o], send_sem=rsend_sem, recv_sem=rrecv_sem.at[q],
-            device_id=peer_from(o), device_id_type=MESH,
-        )
-
+            device_id=(d, from_x[xp] + from_z(p)), device_id_type=MESH,
+        ).start()
+
+    grp = nz // nch
     own = n_exp - 1
 
     def send_chunk(q, carry):
@@ -187,11 +207,7 @@
             fdot(lhs2, rhs2[...]).reshape(oc, 8, LANES).astype(BF)
         )
 
-        def start(i, carry):
-            dispatch(first + i, q).start()
-            return carry
-
-        lax.fori_loop(0, jnp.where(q == nch - 1, oc - 1, oc), start, 0)
+        each_peer(q * grp, q * grp + grp, functools.partial(dispatch, q))
         return carry
 
     lax.fori_loop(0, nch, send_chunk, 0)
@@ -215,11 +231,7 @@
     nt = (((1,), (1,)), ((), ()))
 
     def return_chunk(q):
-        def start(i, carry):
-            give_back(q * oc + i, q).start()
-            return carry
-
-        lax.fori_loop(0, jnp.where(q == nch - 1, oc - 1, oc), start, 0)
+        each_peer(q * grp, q * grp + grp, functools.partial(give_back, q))
 
     def expert_chunk(q, carry):
         first = q * oc

time: 89.9 us -> 89.1 us (level)
  no operation moved by 1% of the time
where the time goes in v3:
time: 89.1 us; the launch traced here: 89 us
  Pallas kernels  88.3 us (99%)
    pallas_call x1, Pallas kernels, local(): pl.pallas_call(functools.partial(kernel, (nz, ny, nch)), out_shape=(jax.S...  86.2 us
    pallas_call x1, Pallas kernels, store(): pl.pallas_call(store_kernel, out_shape=tuple((jax.ShapeDtypeStruct(a.shap...  2.08 us

profile of v3, /device:TPU:1, one launch (start us, length us, event | category | flops | bytes accessed | tf_op | source)
XLA Modules:
  0.0 89.0 jit_solution(311045952298273693)
XLA Ops:
  0.6 86.2 %shard_map.110 = (bf16[128,512]{1,0:T(8,128)(2,1)}, f32[2,128]{1,0:T(2,128)}, bf16[128,512]{1,0:T(8,128)(2,1)}, f32[1,128,512]{2,1,0:T(8,128)}, f32[1,128,512]{2,1,0:T(8,128)}) custom-call(bf16[128,512]{1,0:T(8,128)(2,1)} %tok_hbm.1, f32[1,512]{1,0:T(1,128)} %bitcast.4, s32[2,128]{1,0:T(2,128)} %bitcast.5, f32[2,128]{1,0:T(2,128)} %bitcast.6, ...), custom_call_target="tpu_custom_call" | custom-call | tf_op jit(solution)/shard_map/pallas_call | solution.py:449
  86.9 2.1 %shard_map.111 = (bf16[128,512]{1,0:T(8,128)(2,1)}, f32[2,128]{1,0:T(2,128)}, bf16[128,512]{1,0:T(8,128)(2,1)}, f32[1,128,512]{2,1,0:T(8,128)}, f32[1,128,512]{2,1,0:T(8,128)}) custom-call(bf16[128,512]{1,0:T(8,128)(2,1)} %get-tuple-element.15.refs_0_, f32[2,128]{1,0:T(2,128)} %get-tuple-element.16.refs_1_, bf16[128,512]{1,0:T(8,128)(2,1)} %get-tuple-element.17.refs_2_, ...), custom_call_target="tpu_custom_call" | custom-call | tf_op jit(solution)/shard_map/pallas_call | solution.py:427

commit v4 on v3

--- a/solution.py
+++ b/solution.py
@@ -276,10 +276,6 @@
         return carry
 
     lax.fori_loop(0, nch, expert_chunk, 0)
-    if DELAY:
-        lax.fori_loop(nch - DELAY, nch, lambda q, carry: (return_chunk(q), carry)[1], 0)
-    own_back = pltpu.make_async_copy(rsend.at[own], rrecv.at[own], rrecv_sem.at[nch - 1])
-    own_back.start()
 
     tn = (((0,), (0,)), ((), ()))
 
@@ -313,9 +309,13 @@
 
     hops = []
     grads(0)
+    if DELAY:
+        lax.fori_loop(nch - DELAY, nch, lambda q, carry: (return_chunk(q), carry)[1], 0)
+    own_back = pltpu.make_async_copy(rsend.at[own], rrecv.at[own], rrecv_sem.at[nch - 1])
+    own_back.start()
     for step in range(half):
         js = (0,) if step == 0 else (2 * step - 1, 2 * step)
-        ahead = [j for j in (2 * step + 1, 2 * step + 2) if j < ny]
+        ahead = [j for j in (2 * step, 2 * step + 1) if 0 < j < ny]
         for j in ahead:
             grads(j)
         for j in js:

time: 89.1 us -> 88.9 us (level)
  no operation moved by 1% of the time
where the time goes in v4:
time: 88.9 us; the launch traced here: 88.7 us
  Pallas kernels  88 us (99%)
    pallas_call x1, Pallas kernels, local(): pl.pallas_call(functools.partial(kernel, (nz, ny, nch)), out_shape=(jax.S...  85.9 us
    pallas_call x1, Pallas kernels, store(): pl.pallas_call(store_kernel, out_shape=tuple((jax.ShapeDtypeStruct(a.shap...  2.08 us

profile of v4, /device:TPU:1, one launch (start us, length us, event | category | flops | bytes accessed | tf_op | source)
XLA Modules:
  0.0 88.7 jit_solution(6157543825650571985)
XLA Ops:
  0.6 85.9 %shard_map.110 = (bf16[128,512]{1,0:T(8,128)(2,1)}, f32[2,128]{1,0:T(2,128)}, bf16[128,512]{1,0:T(8,128)(2,1)}, f32[1,128,512]{2,1,0:T(8,128)}, f32[1,128,512]{2,1,0:T(8,128)}) custom-call(bf16[128,512]{1,0:T(8,128)(2,1)} %tok_hbm.1, f32[1,512]{1,0:T(1,128)} %bitcast.4, s32[2,128]{1,0:T(2,128)} %bitcast.5, f32[2,128]{1,0:T(2,128)} %bitcast.6, ...), custom_call_target="tpu_custom_call" | custom-call | tf_op jit(solution)/shard_map/pallas_call | solution.py:449
  86.6 2.1 %shard_map.111 = (bf16[128,512]{1,0:T(8,128)(2,1)}, f32[2,128]{1,0:T(2,128)}, bf16[128,512]{1,0:T(8,128)(2,1)}, f32[1,128,512]{2,1,0:T(8,128)}, f32[1,128,512]{2,1,0:T(8,128)}) custom-call(bf16[128,512]{1,0:T(8,128)(2,1)} %get-tuple-element.15.refs_0_, f32[2,128]{1,0:T(2,128)} %get-tuple-element.16.refs_1_, bf16[128,512]{1,0:T(8,128)(2,1)} %get-tuple-element.17.refs_2_, ...), custom_call_target="tpu_custom_call" | custom-call | tf_op jit(solution)/shard_map/pallas_call | solution.py:427
